TPU v7x, 32 devices: a whole 2x2x4 slice. The times are simulated.
32 devices in a mesh: tier: 4 (over x, core), tile: 8 (over z, y).
Axes of the slice: x: 2, y: 2, z: 4, core: 2. Of those that a mesh axis runs over, the one named last changes fastest.
Arguments:
- starting_warmth_rise: float32 [32, 96, 1024], P('tile', 'tier'), may hold values from -3 to 8
- substance_per_cell: int32 [32, 96, 1024], P('tile', 'tier'), may hold values from 0 to 7
- material_transport_rates: float32 [2, 8], replicated, may hold values from 0.2 to 2
- patch_region_label: int32 [8, 8], P('tile'), may hold values from 0 to 15, as said below
- static_power_per_area: float32 [4, 16], replicated, may hold values from 0.5 to 4
- warming_power_factor: float32 [4, 16], replicated, may hold values from 0.2 to 0.8
- stacking_solve_operator: float32 [96, 96], replicated, may hold values from 0 to 1
Outputs:
- final_temperature: float32 [32, 96, 1024], P('tile', 'tier')
- block_power: float32 [4, 16], P('tier')
Inputs may be any that keep to these rules, and one draw needn't show every extreme that they name: `patch_region_label`: every block number names at least one tile.
All inputs are finite; a program needn't handle non-finite values.
Results may differ from a plain program's by a relative error of at most 0.0001.
Values sent between devices are 32-bit elements; how exact they have to be, the bound alone decides.
A program may use at most 64 MiB of HBM per device.

v0:
```python
import jax
import jax.numpy as jnp
from jax import lax
from jax.sharding import PartitionSpec as P

TILE_COLS = 128
STEPS = 2
LATERAL_RATE = 0.12
SOURCE_GAIN = 0.02


def extended(block, sides, width):
    for axis, dim in sides:
        count = lax.axis_size(axis)
        forward = [(i, i + 1) for i in range(count - 1)]
        backward = [(target, source) for source, target in forward]
        low = lax.ppermute(
            lax.slice_in_dim(block, block.shape[dim] - width, None, axis=dim), axis, forward
        )
        high = lax.ppermute(lax.slice_in_dim(block, 0, width, axis=dim), axis, backward)
        block = jnp.concatenate([low, block, high], axis=dim)
    return block


def pair_mean(cond_a, cond_b):
    return 2.0 * cond_a * cond_b / (cond_a + cond_b)


def lateral(padded, conduct):
    centre = padded[1:-1, :, 1:-1]
    sideways_coupling_rate = conduct[0, 1:-1, :, 1:-1]
    stacking_coupling_rate = conduct[1, 1:-1, :, 1:-1]
    flow_sum = pair_mean(sideways_coupling_rate, conduct[0, 2:, :, 1:-1]) * (
        padded[2:, :, 1:-1] - centre
    )
    flow_sum = flow_sum + pair_mean(sideways_coupling_rate, conduct[0, :-2, :, 1:-1]) * (
        padded[:-2, :, 1:-1] - centre
    )
    flow_sum = flow_sum + pair_mean(stacking_coupling_rate, conduct[1, 1:-1, :, 2:]) * (
        padded[1:-1, :, 2:] - centre
    )
    flow_sum = flow_sum + pair_mean(stacking_coupling_rate, conduct[1, 1:-1, :, :-2]) * (
        padded[1:-1, :, :-2] - centre
    )
    return centre + LATERAL_RATE * flow_sum


def exact_dot(left_op, right_op):
    return jnp.dot(
        left_op, right_op, precision=lax.Precision.HIGHEST, preferred_element_type=jnp.float32
    )


def lookup_codes(codes, material_transport_rates):
    sideways_coupling_rate = jnp.zeros(codes.shape, jnp.float32)
    stacking_coupling_rate = jnp.zeros(codes.shape, jnp.float32)
    for material in range(material_transport_rates.shape[1]):
        is_material = codes == material + 1
        sideways_coupling_rate = jnp.where(
            is_material, material_transport_rates[0, material], sideways_coupling_rate
        )
        stacking_coupling_rate = jnp.where(
            is_material, material_transport_rates[1, material], stacking_coupling_rate
        )
    return jnp.stack([sideways_coupling_rate, stacking_coupling_rate])


def tile_partials(active, tile_hot):
    mesh_height_cells, groups, col_count = active.shape
    quarter = col_count // TILE_COLS
    tile_sums = active.reshape(mesh_height_cells, groups, quarter, TILE_COLS).sum(axis=(0, 3))
    partial_value = exact_dot(tile_sums, tile_hot)
    counts = float(mesh_height_cells * TILE_COLS) * jnp.sum(tile_hot, axis=0)
    return (partial_value, counts)


def spread_power(block_power, tile_hot, mesh_height_cells):
    tile_power = exact_dot(block_power, tile_hot.T)
    groups, quarter = tile_power.shape
    cells = jnp.broadcast_to(
        tile_power[None, :, :, None], (mesh_height_cells, groups, quarter, TILE_COLS)
    )
    return cells.reshape(mesh_height_cells, groups, quarter * TILE_COLS)


def leak_tiers(active, tile_hot, static_power_per_area, warming_power_factor, tier_id):
    partial_value, counts = tile_partials(active, tile_hot)
    block_sum, block_count = lax.psum((partial_value[0], counts), "tile")
    base_row = lax.dynamic_slice_in_dim(static_power_per_area, tier_id, 1, 0)
    slope_row = lax.dynamic_slice_in_dim(warming_power_factor, tier_id, 1, 0)
    return base_row * jnp.exp(slope_row * block_sum[None, :] / block_count[None, :])


def shards(
    starting_warmth_rise,
    substance_per_cell,
    material_transport_rates,
    patch_region_label,
    static_power_per_area,
    warming_power_factor,
    stacking_solve_operator,
):
    mesh_height_cells, stacked_layer_number, lateral_width_cells = starting_warmth_rise.shape
    tier_id = lax.axis_index("tier")
    block_total = static_power_per_area.shape[1]
    codes = substance_per_cell + 1
    block_range = jnp.arange(block_total, dtype=jnp.int32)
    cond_pad = extended(lookup_codes(codes, material_transport_rates), (("tile", 1),), 1)
    cond_pad = jnp.pad(cond_pad, ((0, 0), (0, 0), (0, 0), (1, 1)))
    tile_hot = (patch_region_label[0][:, None] == block_range[None, :]).astype(jnp.float32)
    present_warming_state = starting_warmth_rise
    power_row = jnp.zeros((1, block_total), jnp.float32)
    for step_index in range(STEPS):
        padded = extended(present_warming_state, (("tile", 0),), 1)
        padded = jnp.pad(padded, ((0, 0), (0, 0), (1, 1)))
        power_row = leak_tiers(
            present_warming_state[:, ::stacked_layer_number, :],
            tile_hot,
            static_power_per_area,
            warming_power_factor,
            tier_id,
        )
        moved_field = lateral(padded, cond_pad)
        moved_field = moved_field.at[:, ::stacked_layer_number, :].add(
            SOURCE_GAIN * spread_power(power_row, tile_hot, mesh_height_cells)
        )
        applied = jnp.einsum(
            "lm,rmc->rlc",
            stacking_solve_operator,
            lax.all_to_all(moved_field, "tier", split_axis=2, concat_axis=1, tiled=True),
            precision=lax.Precision.HIGHEST,
        )
        present_warming_state = lax.all_to_all(
            applied, "tier", split_axis=1, concat_axis=2, tiled=True
        )
    return (present_warming_state, power_row)


def solution(mesh):
    in_specs = (
        P("tile", "tier", None),
        P("tile", "tier", None),
        P(),
        P("tile", None),
        P(),
        P(),
        P(),
    )
    out_specs = (P("tile", "tier", None), P("tier", None))
    return jax.shard_map(shards, mesh=mesh, in_specs=in_specs, out_specs=out_specs, check_vma=False)
```

profile of v0, /device:TPU:8, one launch (start us, length us, event | category | flops | bytes accessed | tf_op | source)
XLA Modules:
  0.0 144.2 jit_solution(3918848064363869905)
XLA Ops:
  0.6 1.0 fusion.41
  1.6 3.4 %collective-permute-start.3 = (f32[1,24,1024]{2,1,0:T(8,128)S(1)}, f32[1,24,1024]{2,1,0:T(8,128)S(1)}, u32[]{:S(2)}, u32[]{:S(2)}) collective-permute-start(f32[1,24,1024]{2,1,0:T(8,128)S(1)} %get-tuple-element.44), channel_id=1, source_target_pairs={{0,1},{1,2},{2,3},{3,4},{4,5},{5,6},{6,7},{8,9},{9,10},{10,11},{11... | collective-permute-start | bytes 294920 | tf_op jit(solution)/shard_map/ppermute | solution.py:17
  5.0 3.3 %collective-permute-start.1 = (f32[1,24,1024]{2,1,0:T(8,128)S(1)}, f32[1,24,1024]{2,1,0:T(8,128)S(1)}, u32[]{:S(2)}, u32[]{:S(2)}) collective-permute-start(f32[1,24,1024]{2,1,0:T(8,128)S(1)} %get-tuple-element.45), channel_id=1, source_target_pairs={{1,0},{2,1},{3,2},{4,3},{5,4},{6,5},{7,6},{9,8},{10,9},{11,10},{12... | collective-permute-start | bytes 294920 | tf_op jit(solution)/shard_map/ppermute | solution.py:20
  8.4 2.0 %fusion.42 = (f32[1,1]{1,0:T(1,128)}, f32[1,1]{1,0:T(1,128)}, f32[1,1]{1,0:T(1,128)}, f32[1,1]{1,0:T(1,128)}, f32[1,1]{1,0:T(1,128)}, /*index=5*/f32[1,1]{1,0:T(...) fusion(f32[2,8]{1,0:T(2,128)} %param.13), kind=kLoop, calls=%fused_computation.105 | loop fusion | bytes 128 | tf_op jit(solution)/shard_map/slice | solution.py:60
  10.3 6.6 %select_select_fusion = (f32[4,24,1024]{2,1,0:T(8,128)S(1)}, pred[4,24,1024]{2,1,0:T(8,128)(4,1)S(1)}, pred[4,24,1024]{2,1,0:T(8,128)(4,1)S(1)}, pred[4,24,1024]...) fusion(f32[]{:T(128)} %bitcast.16, f32[]{:T(128)} %bitcast.15, ...), kind=kLoop, calls=%fused_computation.62 | loop fusion | flops 1671168 | bytes 1572896 | tf_op jit(solution)/shard_map/jit(_where)/select_n | solution.py:62
  17.0 5.4 %select_select_fusion.1 = f32[4,24,1024]{2,1,0:T(8,128)S(1)} fusion(pred[4,24,1024]{2,1,0:T(8,128)(4,1)S(1)} %get-tuple-element.39, pred[4,24,1024]{2,1,0:T(8,128)(4,1)S(1)} %get-tuple-element.38, pred[4,24,1024]{2,1,0:T(8,128)(4,1)S(1)} %get-tuple-element.37, pred[4,24,1024]{2,1,0:T(8,128)(4,1)S(1)} %get-tuple-element.36, ...), kind=kLoop, calls=%fused_computation.63 | loop fusion | flops 786432 | bytes 1179680 | tf_op jit(solution)/shard_map/jit(_where)/select_n | solution.py:59
  22.4 2.5 %collective-permute-start.2 = (f32[2,1,24,1024]{3,2,1,0:T(8,128)S(1)}, f32[2,1,24,1024]{3,2,1,0:T(8,128)S(1)}, u32[]{:S(2)}, u32[]{:S(2)}) collective-permute-start(f32[2,1,24,1024]{3,2,1,0:T(8,128)S(1)} %get-tuple-element.40), channel_id=1, source_target_pairs={{0,1},{1,2},{2,3},{3,4},{4,5},{5,6},{6,7},{8,9},{9,10},{10,11},{11... | collective-permute-start | bytes 589832 | tf_op jit(solution)/shard_map/ppermute | solution.py:17
  24.9 4.2 %collective-permute-start = (f32[2,1,24,1024]{3,2,1,0:T(8,128)S(1)}, f32[2,1,24,1024]{3,2,1,0:T(8,128)S(1)}, u32[]{:S(2)}, u32[]{:S(2)}) collective-permute-start(f32[2,1,24,1024]{3,2,1,0:T(8,128)S(1)} %get-tuple-element.41), channel_id=1, source_target_pairs={{1,0},{2,1},{3,2},{4,3},{5,4},{6,5},{7,6},{9,8},{10,9},{11,10},{12... | collective-permute-start | bytes 589832 | tf_op jit(solution)/shard_map/ppermute | solution.py:20
  29.4 0.2 fusion.31
  29.6 17.1 %all-reduce.3 = (f32[1,16]{1,0:T(1,128)S(1)}, f32[1,16]{1,0:T(1,128)S(1)}) all-reduce(f32[1,16]{1,0:T(1,128)S(1)} %multiply_bitcast_fusion.2, f32[1,16]{1,0:T(1,128)S(1)} %fusion.31), channel_id=1, replica_groups=mesh['tier'=4,'tile'=8] {'tile'}, use_global_device_ids=true, to_apply=%region_4.5 | all-reduce | flops 32 | bytes 256 | tf_op jit(solution)/shard_map/psum | solution.py:88
  46.7 0.2 fusion.1
  46.9 0.3 select_maximum_fusion.5
  47.2 0.4 select_maximum_fusion
  47.6 1.2 fusion.18
  48.9 0.1 scatter-add.6
  49.0 0.9 copy.88
  49.9 2.9 %reshape.124 = f32[4,1,24576]{2,1,0:T(1,128)S(1)} reshape(f32[1024,4,24]{2,1,0:T(4,128)S(1)} %bitcast.115) | data formatting | bytes 786432
  52.8 10.0 %all_to_all.72 = f32[4,1,24576]{2,1,0:T(1,128)S(1)} all-to-all(f32[4,1,24576]{2,1,0:T(1,128)S(1)} %reshape.124), channel_id=1, replica_groups=mesh['tier'=4,'tile'=8] {'tier'}, dimensions={0} | all-to-all | bytes 786432 | tf_op jit(solution)/shard_map/all_to_all | solution.py:130
  62.8 0.5 broadcast.157
  63.3 1.7 %reduce.10 = f32[4,24576]{1,0:T(4,128)S(1)} reduce(f32[4,1,24576]{2,1,0:T(1,128)S(1)} %all_to_all.72, f32[]{:T(128)} %broadcast.157), dimensions={1}, to_apply=%all_to_all.52.reduce_sub_computation | reduce | bytes 786436 | tf_op jit(solution)/shard_map/all_to_all | solution.py:130
  65.0 2.8 %reshape.125 = f32[1024,4,24]{2,1,0:T(4,128)S(1)} reshape(f32[4,24576]{1,0:T(4,128)S(1)} %reduce.10) | data formatting | bytes 786432
  67.8 0.8 copy.89
  68.6 0.5 convolution_bitcast_fusion.1
  69.1 0.3 copy.90
  69.4 9.8 %all_to_all.73 = f32[4,96,256]{2,0,1:T(4,128)S(1)} all-to-all(f32[4,96,256]{2,0,1:T(4,128)S(1)} %copy.90), channel_id=1, replica_groups=mesh['tier'=4,'tile'=8] {'tier'}, dimensions={1} | all-to-all | bytes 786432 | tf_op jit(solution)/shard_map/all_to_all | solution.py:133
  79.2 0.3 copy.97
  79.5 0.2 all_to_all.59
  79.8 0.2 fusion.30
  80.1 17.1 %psum.26 = f32[1,16]{1,0:T(1,128)S(1)} all-reduce(f32[1,16]{1,0:T(1,128)S(1)} %fusion.30), channel_id=1, replica_groups=mesh['tier'=4,'tile'=8] {'tile'}, use_global_device_ids=true, to_apply=%region_7.8 | all-reduce | flops 16 | bytes 128 | tf_op jit(solution)/shard_map/psum | solution.py:88
  97.2 0.2 fusion.2
  97.5 6.6 %collective-permute-start.4 = (f32[1,24,1024]{2,1,0:T(8,128)S(1)}, f32[1,24,1024]{2,1,0:T(8,128)S(1)}, u32[]{:S(2)}, u32[]{:S(2)}) collective-permute-start(f32[1,24,1024]{2,1,0:T(8,128)S(1)} %slice.219), channel_id=1, source_target_pairs={{1,0},{2,1},{3,2},{4,3},{5,4},{6,5},{7,6},{9,8},{10,9},{11,10},{12... | collective-permute-start | bytes 294920 | tf_op jit(solution)/shard_map/ppermute | solution.py:20
  104.1 1.9 %collective-permute-start.5 = (f32[1,24,1024]{2,1,0:T(8,128)S(1)}, f32[1,24,1024]{2,1,0:T(8,128)S(1)}, u32[]{:S(2)}, u32[]{:S(2)}) collective-permute-start(f32[1,24,1024]{2,1,0:T(8,128)S(1)} %slice.222), channel_id=1, source_target_pairs={{0,1},{1,2},{2,3},{3,4},{4,5},{5,6},{6,7},{8,9},{9,10},{10,11},{11... | collective-permute-start | bytes 294920 | tf_op jit(solution)/shard_map/ppermute | solution.py:17
  106.1 0.2 collective-permute-done.4
  106.3 5.2 %collective-permute-done.5 = f32[1,24,1024]{2,1,0:T(8,128)S(1)} collective-permute-done((f32[1,24,1024]{2,1,0:T(8,128)S(1)}, f32[1,24,1024]{2,1,0:T(8,128)S(1)}, u32[]{:S(2)}, u32[]{:S(2)}) %collective-permute-start.5) | collective-permute-done | bytes 98336 | tf_op jit(solution)/shard_map/ppermute | solution.py:17
  111.5 0.2 select_maximum_fusion.3
  111.8 1.4 fusion.7
  113.2 0.3 scatter-add.9
  113.5 0.9 copy.92
  114.4 2.9 %reshape.126 = f32[4,1,24576]{2,1,0:T(1,128)S(1)} reshape(f32[1024,4,24]{2,1,0:T(4,128)S(1)} %bitcast.117) | data formatting | bytes 786432
  117.3 9.8 %all_to_all.74 = f32[4,1,24576]{2,1,0:T(1,128)S(1)} all-to-all(f32[4,1,24576]{2,1,0:T(1,128)S(1)} %reshape.126), channel_id=1, replica_groups=mesh['tier'=4,'tile'=8] {'tier'}, dimensions={0} | all-to-all | bytes 786432 | tf_op jit(solution)/shard_map/all_to_all | solution.py:130
  127.1 1.7 %reduce.11 = f32[4,24576]{1,0:T(4,128)S(1)} reduce(f32[4,1,24576]{2,1,0:T(1,128)S(1)} %all_to_all.74, f32[]{:T(128)} %broadcast.157), dimensions={1}, to_apply=%all_to_all.60.reduce_sub_computation | reduce | bytes 786436 | tf_op jit(solution)/shard_map/all_to_all | solution.py:130
  128.8 2.8 %reshape.127 = f32[1024,4,24]{2,1,0:T(4,128)S(1)} reshape(f32[4,24576]{1,0:T(4,128)S(1)} %reduce.11) | data formatting | bytes 786432
  131.6 0.8 copy.93
  132.4 0.5 convolution_bitcast_fusion
  132.9 0.3 copy.94
  133.2 9.8 %all_to_all.75 = f32[4,96,256]{2,0,1:T(4,128)S(1)} all-to-all(f32[4,96,256]{2,0,1:T(4,128)S(1)} %copy.94), channel_id=1, replica_groups=mesh['tier'=4,'tile'=8] {'tier'}, dimensions={1} | all-to-all | bytes 786432 | tf_op jit(solution)/shard_map/all_to_all | solution.py:133
  143.0 0.3 copy.95
  143.3 0.9 all_to_all.67
  (35 shorter events, 0.7 us)
Async XLA Ops:
  0.6 68.0 %copy-start = (f32[96,96]{1,0:T(8,128)S(1)}, f32[96,96]{1,0:T(8,128)}, u32[]{:S(2)}) copy-start(f32[96,96]{1,0:T(8,128)} %param.17) | copy-start | bytes 110596
  1.6 45.3 %collective-permute-start.3 = (f32[1,24,1024]{2,1,0:T(8,128)S(1)}, f32[1,24,1024]{2,1,0:T(8,128)S(1)}, u32[]{:S(2)}, u32[]{:S(2)}) collective-permute-start(f32[1,24,1024]{2,1,0:T(8,128)S(1)} %get-tuple-element.44), channel_id=1, source_target_pairs={{0,1},{1,2},{2,3},{3,4},{4,5},{5,6},{6,7},{8,9},{9,10},{10,11},{11... | collective-permute-start | bytes 294920 | tf_op jit(solution)/shard_map/ppermute | solution.py:17
  5.0 41.9 %collective-permute-start.1 = (f32[1,24,1024]{2,1,0:T(8,128)S(1)}, f32[1,24,1024]{2,1,0:T(8,128)S(1)}, u32[]{:S(2)}, u32[]{:S(2)}) collective-permute-start(f32[1,24,1024]{2,1,0:T(8,128)S(1)} %get-tuple-element.45), channel_id=1, source_target_pairs={{1,0},{2,1},{3,2},{4,3},{5,4},{6,5},{7,6},{9,8},{10,9},{11,10},{12... | collective-permute-start | bytes 294920 | tf_op jit(solution)/shard_map/ppermute | solution.py:20
  16.9 12.2 %copy-start.3 = (f32[4,24,1024]{2,1,0:T(8,128)S(1)}, f32[4,24,1024]{2,1,0:T(8,128)}, u32[]{:S(2)}) copy-start(f32[4,24,1024]{2,1,0:T(8,128)} %param.11) | copy-start | bytes 1179652
  16.9 12.2 %copy-start.7 = (s32[1,8]{1,0:T(1,128)S(1)}, s32[1,8]{1,0:T(1,128)}, u32[]{:S(2)}) copy-start(s32[1,8]{1,0:T(1,128)} %param.14) | copy-start | bytes 100
  16.9 29.7 %copy-start.5 = (f32[4,16]{1,0:T(4,128)S(1)}, f32[4,16]{1,0:T(4,128)}, u32[]{:S(2)}) copy-start(f32[4,16]{1,0:T(4,128)} %param.15) | copy-start | bytes 772
  16.9 29.7 %copy-start.6 = (f32[4,16]{1,0:T(4,128)S(1)}, f32[4,16]{1,0:T(4,128)}, u32[]{:S(2)}) copy-start(f32[4,16]{1,0:T(4,128)} %param.16) | copy-start | bytes 772
  22.4 24.8 %collective-permute-start.2 = (f32[2,1,24,1024]{3,2,1,0:T(8,128)S(1)}, f32[2,1,24,1024]{3,2,1,0:T(8,128)S(1)}, u32[]{:S(2)}, u32[]{:S(2)}) collective-permute-start(f32[2,1,24,1024]{3,2,1,0:T(8,128)S(1)} %get-tuple-element.40), channel_id=1, source_target_pairs={{0,1},{1,2},{2,3},{3,4},{4,5},{5,6},{6,7},{8,9},{9,10},{10,11},{11... | collective-permute-start | bytes 589832 | tf_op jit(solution)/shard_map/ppermute | solution.py:17
  24.9 22.3 %collective-permute-start = (f32[2,1,24,1024]{3,2,1,0:T(8,128)S(1)}, f32[2,1,24,1024]{3,2,1,0:T(8,128)S(1)}, u32[]{:S(2)}, u32[]{:S(2)}) collective-permute-start(f32[2,1,24,1024]{3,2,1,0:T(8,128)S(1)} %get-tuple-element.41), channel_id=1, source_target_pairs={{1,0},{2,1},{3,2},{4,3},{5,4},{6,5},{7,6},{9,8},{10,9},{11,10},{12... | collective-permute-start | bytes 589832 | tf_op jit(solution)/shard_map/ppermute | solution.py:20
  47.6 1.3 copy-start.1
  79.5 32.3 %copy-start.2 = (f32[2,6,24,1026]{3,2,1,0:T(8,128)S(1)}, f32[2,6,24,1026]{3,2,1,0:T(8,128)}, u32[]{:S(2)}) copy-start(f32[2,6,24,1026]{3,2,1,0:T(8,128)} %copy-done.1) | copy-start | bytes 3545860
  97.2 16.0 %copy-start.4 = (f32[1,16]{1,0:T(1,128)}, f32[1,16]{1,0:T(1,128)S(1)}, u32[]{:S(2)}) copy-start(f32[1,16]{1,0:T(1,128)S(1)} %exponential_multiply_fusion) | copy-start | bytes 196
  97.5 8.8 %collective-permute-start.4 = (f32[1,24,1024]{2,1,0:T(8,128)S(1)}, f32[1,24,1024]{2,1,0:T(8,128)S(1)}, u32[]{:S(2)}, u32[]{:S(2)}) collective-permute-start(f32[1,24,1024]{2,1,0:T(8,128)S(1)} %slice.219), channel_id=1, source_target_pairs={{1,0},{2,1},{3,2},{4,3},{5,4},{6,5},{7,6},{9,8},{10,9},{11,10},{12... | collective-permute-start | bytes 294920 | tf_op jit(solution)/shard_map/ppermute | solution.py:20
  104.1 7.4 %collective-permute-start.5 = (f32[1,24,1024]{2,1,0:T(8,128)S(1)}, f32[1,24,1024]{2,1,0:T(8,128)S(1)}, u32[]{:S(2)}, u32[]{:S(2)}) collective-permute-start(f32[1,24,1024]{2,1,0:T(8,128)S(1)} %slice.222), channel_id=1, source_target_pairs={{0,1},{1,2},{2,3},{3,4},{4,5},{5,6},{6,7},{8,9},{9,10},{10,11},{11... | collective-permute-start | bytes 294920 | tf_op jit(solution)/shard_map/ppermute | solution.py:17
where the time goes:
time: 145 us; the launch traced here: 144 us
  blocking collectives  73.7 us (51%)
  starting transfers between devices  22 us (15%)
  local copies, waits for them, and re-layouts  21 us (14%)
  other arithmetic  19.3 us (13%)
  waiting for transfers between devices  5.42 us (4%)
  matrix products  1.71 us (1%)
    psum x2, blocking collectives, leak_tiers(): block_sum, block_count = lax.psum((partial_value[0], counts), 'tile')  34.2 us
    all_to_all x2, blocking collectives, shards(): lax.all_to_all(moved_field, 'tier', split_axis=2, concat_axis=1, tiled=True)  19.8 us
    all_to_all x2, blocking collectives, shards(): lax.all_to_all(applied, 'tier', split_axis=1, concat_axis=2, tiled=True)  19.7 us
    ppermute x3, starting transfers between devices, extended(): lax.ppermute(lax.slice_in_dim(block, 0, width, axis=dim), axis, backward)  14.1 us
    unnamed x20, local copies, waits for them, and re-layouts  11.4 us
    ppermute x3, starting transfers between devices, extended(): lax.ppermute(lax.slice_in_dim(block, block.shape[dim] - width, None, axis...  7.88 us
    select_n x1, other arithmetic, lookup_codes(): jnp.where(is_material, material_transport_rates[1, material], stacking_co...  6.55 us
    select_n x1, other arithmetic, lookup_codes(): jnp.where(is_material, material_transport_rates[0, material], sideways_co...  5.36 us
  transfers between devices with their start and end apart: 6, of which 2 were waited for; matrix products, arithmetic and copies ran while one was open for 10% of the time, Pallas kernels for 0%

commit v1 on v0

--- a/solution.py
+++ b/solution.py
@@ -130,9 +130,9 @@
             lax.all_to_all(moved_field, "tier", split_axis=2, concat_axis=1, tiled=True),
             precision=lax.Precision.HIGHEST,
         )
-        present_warming_state = lax.all_to_all(
-            applied, "tier", split_axis=1, concat_axis=2, tiled=True
-        )
+        pieces = jnp.split(applied, lax.axis_size("tier"), axis=1)
+        incoming = lax.all_to_all(jnp.stack(pieces), "tier", 0, 0)
+        present_warming_state = jnp.concatenate(incoming, axis=2)
     return (present_warming_state, power_row)
 
 

time: 145 us -> 140 us (0.966)
  the two profiles are of different devices: /device:TPU:8 before, /device:TPU:0 now
where the time goes in v1:
time: 140 us
  blocking collectives  79.9 us (57%)
  local copies, waits for them, and re-layouts  19.6 us (14%)
  other arithmetic  19.4 us (14%)
  starting transfers between devices  18 us (13%)
  matrix products  1.71 us (1%)
    psum x2, blocking collectives, leak_tiers(): block_sum, block_count = lax.psum((partial_value[0], counts), 'tile')  40.4 us
    all_to_all x2, blocking collectives, shards(): lax.all_to_all(moved_field, 'tier', split_axis=2, concat_axis=1, tiled=True)  19.8 us
    all_to_all x2, blocking collectives, shards(): incoming = lax.all_to_all(jnp.stack(pieces), 'tier', 0, 0)  19.7 us
    ppermute x3, starting transfers between devices, extended(): lax.ppermute(lax.slice_in_dim(block, block.shape[dim] - width, None, axis...  14 us
    unnamed x21, local copies, waits for them, and re-layouts  11.4 us
    select_n x1, other arithmetic, lookup_codes(): jnp.where(is_material, material_transport_rates[1, material], stacking_co...  6.55 us
    select_n x1, other arithmetic, lookup_codes(): jnp.where(is_material, material_transport_rates[0, material], sideways_co...  5.36 us
    ppermute x3, starting transfers between devices, extended(): lax.ppermute(lax.slice_in_dim(block, 0, width, axis=dim), axis, backward)  4.01 us
  transfers between devices with their start and end apart: 6, of which 0 were waited for; matrix products, arithmetic and copies ran while one was open for 11% of the time, Pallas kernels for 0%

profile of v1, /device:TPU:0, one launch (start us, length us, event | category | flops | bytes accessed | tf_op | source)
XLA Modules:
  0.0 139.7 jit_solution(6274307665839104735)
XLA Ops:
  0.6 0.0 copy-start
  0.6 1.0 fusion.40
  1.6 4.9 %collective-permute-start.3 = (f32[1,24,1024]{2,1,0:T(8,128)S(1)}, f32[1,24,1024]{2,1,0:T(8,128)S(1)}, u32[]{:S(2)}, u32[]{:S(2)}) collective-permute-start(f32[1,24,1024]{2,1,0:T(8,128)S(1)} %get-tuple-element.52), channel_id=1, source_target_pairs={{0,1},{1,2},{2,3},{3,4},{4,5},{5,6},{6,7},{8,9},{9,10},{10,11},{11... | collective-permute-start | bytes 294920 | tf_op jit(solution)/shard_map/ppermute | solution.py:17
  6.5 1.3 collective-permute-start.1
  7.8 2.0 %fusion.41 = (f32[1,1]{1,0:T(1,128)}, f32[1,1]{1,0:T(1,128)}, f32[1,1]{1,0:T(1,128)}, f32[1,1]{1,0:T(1,128)}, f32[1,1]{1,0:T(1,128)}, /*index=5*/f32[1,1]{1,0:T(...) fusion(f32[2,8]{1,0:T(2,128)} %param.13), kind=kLoop, calls=%fused_computation.115 | loop fusion | bytes 128 | tf_op jit(solution)/shard_map/slice | solution.py:60
  9.8 6.6 %select_select_fusion = (f32[4,24,1024]{2,1,0:T(8,128)S(1)}, pred[4,24,1024]{2,1,0:T(8,128)(4,1)S(1)}, pred[4,24,1024]{2,1,0:T(8,128)(4,1)S(1)}, pred[4,24,1024]...) fusion(f32[]{:T(128)} %bitcast.16, f32[]{:T(128)} %bitcast.15, ...), kind=kLoop, calls=%fused_computation.63 | loop fusion | flops 1671168 | bytes 1572896 | tf_op jit(solution)/shard_map/jit(_where)/select_n | solution.py:62
  16.3 0.0 copy-start.3
  16.4 5.4 %select_select_fusion.1 = f32[4,24,1024]{2,1,0:T(8,128)S(1)} fusion(pred[4,24,1024]{2,1,0:T(8,128)(4,1)S(1)} %get-tuple-element.39, pred[4,24,1024]{2,1,0:T(8,128)(4,1)S(1)} %get-tuple-element.38, pred[4,24,1024]{2,1,0:T(8,128)(4,1)S(1)} %get-tuple-element.37, pred[4,24,1024]{2,1,0:T(8,128)(4,1)S(1)} %get-tuple-element.36, ...), kind=kLoop, calls=%fused_computation.64 | loop fusion | flops 786432 | bytes 1179680 | tf_op jit(solution)/shard_map/jit(_where)/select_n | solution.py:59
  21.8 4.6 %collective-permute-start.2 = (f32[2,1,24,1024]{3,2,1,0:T(8,128)S(1)}, f32[2,1,24,1024]{3,2,1,0:T(8,128)S(1)}, u32[]{:S(2)}, u32[]{:S(2)}) collective-permute-start(f32[2,1,24,1024]{3,2,1,0:T(8,128)S(1)} %get-tuple-element.40), channel_id=1, source_target_pairs={{0,1},{1,2},{2,3},{3,4},{4,5},{5,6},{6,7},{8,9},{9,10},{10,11},{11... | collective-permute-start | bytes 589832 | tf_op jit(solution)/shard_map/ppermute | solution.py:17
  26.3 1.3 collective-permute-start
  27.7 0.1 convert_reduce_fusion
  27.8 0.1 bitcast_reduce_fusion.1
  27.9 0.2 fusion.31
  28.1 22.8 %all-reduce.3 = (f32[1,16]{1,0:T(1,128)S(1)}, f32[1,16]{1,0:T(1,128)S(1)}) all-reduce(f32[1,16]{1,0:T(1,128)S(1)} %multiply_bitcast_fusion.2, f32[1,16]{1,0:T(1,128)S(1)} %fusion.31), channel_id=1, replica_groups=mesh['tier'=4,'tile'=8] {'tile'}, use_global_device_ids=true, to_apply=%region_4.5 | all-reduce | flops 32 | bytes 256 | tf_op jit(solution)/shard_map/psum | solution.py:88
  50.9 0.2 fusion.1
  51.1 0.1 broadcast_bitcast_fusion.1
  51.2 0.3 select_maximum_fusion.5
  51.4 0.4 select_maximum_fusion
  51.9 1.2 fusion.18
  53.1 0.1 scatter-add.6
  53.3 0.9 copy.25
  54.1 2.9 %reshape.140 = f32[4,1,24576]{2,1,0:T(1,128)S(1)} reshape(f32[1024,4,24]{2,1,0:T(4,128)S(1)} %bitcast.136) | data formatting | bytes 786432
  57.0 10.0 %all_to_all.46 = f32[4,1,24576]{2,1,0:T(1,128)S(1)} all-to-all(f32[4,1,24576]{2,1,0:T(1,128)S(1)} %reshape.140), channel_id=1, replica_groups=mesh['tier'=4,'tile'=8] {'tier'}, dimensions={0} | all-to-all | bytes 786432 | tf_op jit(solution)/shard_map/all_to_all | solution.py:130
  67.0 0.5 broadcast.157
  67.5 1.7 %reduce.10 = f32[4,24576]{1,0:T(4,128)S(1)} reduce(f32[4,1,24576]{2,1,0:T(1,128)S(1)} %all_to_all.46, f32[]{:T(128)} %broadcast.157), dimensions={1}, to_apply=%all_to_all.32.reduce_sub_computation | reduce | bytes 786436 | tf_op jit(solution)/shard_map/all_to_all | solution.py:130
  69.3 2.8 %reshape.141 = f32[1024,4,24]{2,1,0:T(4,128)S(1)} reshape(f32[4,24576]{1,0:T(4,128)S(1)} %reduce.10) | data formatting | bytes 786432
  72.1 0.8 copy.26
  72.8 0.5 convolution_bitcast_fusion.1
  73.4 9.8 %all_to_all.47 = f32[4,4,24,256]{3,2,1,0:T(8,128)S(1)} all-to-all(f32[4,4,24,256]{3,2,1,0:T(8,128)S(1)} %pad_maximum_fusion.8), channel_id=1, replica_groups=mesh['tier'=4,'tile'=8] {'tier'}, dimensions={0} | all-to-all | bytes 786432 | tf_op jit(solution)/shard_map/all_to_all | solution.py:134
  83.3 1.4 %collective-permute-start.4 = (f32[1,24,1024]{2,1,0:T(8,128)S(1)}, f32[1,24,1024]{2,1,0:T(8,128)S(1)}, u32[]{:S(2)}, u32[]{:S(2)}) collective-permute-start(f32[1,24,1024]{2,1,0:T(8,128)S(1)} %bitcast.150), channel_id=1, source_target_pairs={{1,0},{2,1},{3,2},{4,3},{5,4},{6,5},{7,6},{9,8},{10,9},{11,10},{12... | collective-permute-start | bytes 294920 | tf_op jit(solution)/shard_map/ppermute | solution.py:20
  84.8 0.1 bitcast_reduce_fusion
  84.9 0.2 fusion.30
  85.1 4.5 %collective-permute-start.5 = (f32[1,24,1024]{2,1,0:T(8,128)S(1)}, f32[1,24,1024]{2,1,0:T(8,128)S(1)}, u32[]{:S(2)}, u32[]{:S(2)}) collective-permute-start(f32[1,24,1024]{2,1,0:T(8,128)S(1)} %bitcast.149), channel_id=1, source_target_pairs={{0,1},{1,2},{2,3},{3,4},{4,5},{5,6},{6,7},{8,9},{9,10},{10,11},{11... | collective-permute-start | bytes 294920 | tf_op jit(solution)/shard_map/ppermute | solution.py:17
  89.7 17.6 %psum.26 = f32[1,16]{1,0:T(1,128)S(1)} all-reduce(f32[1,16]{1,0:T(1,128)S(1)} %fusion.30), channel_id=1, replica_groups=mesh['tier'=4,'tile'=8] {'tile'}, use_global_device_ids=true, to_apply=%region_7.8 | all-reduce | flops 16 | bytes 128 | tf_op jit(solution)/shard_map/psum | solution.py:88
  107.3 0.2 fusion.2
  107.5 0.1 broadcast_bitcast_fusion
  107.6 0.2 select_maximum_fusion.3
  107.9 1.4 %fusion.7 = f32[4,24,1024]{2,1,0:T(8,128)S(1)} fusion(f32[4,24,1024]{2,1,0:T(8,128)S(1)} %bitcast.142, f32[6,24,1026]{2,1,0:T(8,128)S(1)} %select_maximum_fusion.3, f32[4,24,1024]{2,1,0:T(8,128)} %get-tuple-element.30, f32[1,24,1024]{2,1,0:T(8,128)S(1)} %collective-permute-done.5, f32[4,24,1024]{2,1,0:T(8,128)S(1)} %get-tuple-element.29, ...), kind=kLoop, calls=%fused_computation.23 | loop fusion | flops 2162688 | bytes 3735552 | tf_op jit(solution)/shard_map/add | solution.py:45
  109.3 0.3 scatter-add.9
  109.6 0.9 copy.30
  110.5 2.9 %reshape.142 = f32[4,1,24576]{2,1,0:T(1,128)S(1)} reshape(f32[1024,4,24]{2,1,0:T(4,128)S(1)} %bitcast.138) | data formatting | bytes 786432
  113.4 9.8 %all_to_all.48 = f32[4,1,24576]{2,1,0:T(1,128)S(1)} all-to-all(f32[4,1,24576]{2,1,0:T(1,128)S(1)} %reshape.142), channel_id=1, replica_groups=mesh['tier'=4,'tile'=8] {'tier'}, dimensions={0} | all-to-all | bytes 786432 | tf_op jit(solution)/shard_map/all_to_all | solution.py:130
  123.2 1.7 %reduce.11 = f32[4,24576]{1,0:T(4,128)S(1)} reduce(f32[4,1,24576]{2,1,0:T(1,128)S(1)} %all_to_all.48, f32[]{:T(128)} %broadcast.157), dimensions={1}, to_apply=%all_to_all.37.reduce_sub_computation | reduce | bytes 786436 | tf_op jit(solution)/shard_map/all_to_all | solution.py:130
  124.9 2.8 %reshape.143 = f32[1024,4,24]{2,1,0:T(4,128)S(1)} reshape(f32[4,24576]{1,0:T(4,128)S(1)} %reduce.11) | data formatting | bytes 786432
  127.7 0.8 copy.31
  128.5 0.5 convolution_bitcast_fusion
  129.1 9.8 %all_to_all.49 = f32[4,4,24,256]{3,2,1,0:T(8,128)S(1)} all-to-all(f32[4,4,24,256]{3,2,1,0:T(8,128)S(1)} %pad_maximum_fusion.9), channel_id=1, replica_groups=mesh['tier'=4,'tile'=8] {'tier'}, dimensions={0} | all-to-all | bytes 786432 | tf_op jit(solution)/shard_map/all_to_all | solution.py:134
  138.9 0.8 copy.36
  (35 shorter events, 0.3 us)
Async XLA Ops:
  0.6 72.2 %copy-start = (f32[96,96]{1,0:T(8,128)S(1)}, f32[96,96]{1,0:T(8,128)}, u32[]{:S(2)}) copy-start(f32[96,96]{1,0:T(8,128)} %param.17) | copy-start | bytes 110596
  1.6 49.5 %collective-permute-start.3 = (f32[1,24,1024]{2,1,0:T(8,128)S(1)}, f32[1,24,1024]{2,1,0:T(8,128)S(1)}, u32[]{:S(2)}, u32[]{:S(2)}) collective-permute-start(f32[1,24,1024]{2,1,0:T(8,128)S(1)} %get-tuple-element.52), channel_id=1, source_target_pairs={{0,1},{1,2},{2,3},{3,4},{4,5},{5,6},{6,7},{8,9},{9,10},{10,11},{11... | collective-permute-start | bytes 294920 | tf_op jit(solution)/shard_map/ppermute | solution.py:17
  6.5 44.7 %collective-permute-start.1 = (f32[1,24,1024]{2,1,0:T(8,128)S(1)}, f32[1,24,1024]{2,1,0:T(8,128)S(1)}, u32[]{:S(2)}, u32[]{:S(2)}) collective-permute-start(f32[1,24,1024]{2,1,0:T(8,128)S(1)} %get-tuple-element.53), channel_id=1, source_target_pairs={{1,0},{2,1},{3,2},{4,3},{5,4},{6,5},{7,6},{9,8},{10,9},{11,10},{12... | collective-permute-start | bytes 294920 | tf_op jit(solution)/shard_map/ppermute | solution.py:20
  16.3 11.3 %copy-start.3 = (f32[4,24,1024]{2,1,0:T(8,128)S(1)}, f32[4,24,1024]{2,1,0:T(8,128)}, u32[]{:S(2)}) copy-start(f32[4,24,1024]{2,1,0:T(8,128)} %param.11) | copy-start | bytes 1179652
  16.3 11.3 %copy-start.7 = (s32[1,8]{1,0:T(1,128)S(1)}, s32[1,8]{1,0:T(1,128)}, u32[]{:S(2)}) copy-start(s32[1,8]{1,0:T(1,128)} %param.14) | copy-start | bytes 100
  16.4 34.5 %copy-start.5 = (f32[4,16]{1,0:T(4,128)S(1)}, f32[4,16]{1,0:T(4,128)}, u32[]{:S(2)}) copy-start(f32[4,16]{1,0:T(4,128)} %param.15) | copy-start | bytes 772
  16.4 34.5 %copy-start.6 = (f32[4,16]{1,0:T(4,128)S(1)}, f32[4,16]{1,0:T(4,128)}, u32[]{:S(2)}) copy-start(f32[4,16]{1,0:T(4,128)} %param.16) | copy-start | bytes 772
  21.8 29.6 %collective-permute-start.2 = (f32[2,1,24,1024]{3,2,1,0:T(8,128)S(1)}, f32[2,1,24,1024]{3,2,1,0:T(8,128)S(1)}, u32[]{:S(2)}, u32[]{:S(2)}) collective-permute-start(f32[2,1,24,1024]{3,2,1,0:T(8,128)S(1)} %get-tuple-element.40), channel_id=1, source_target_pairs={{0,1},{1,2},{2,3},{3,4},{4,5},{5,6},{6,7},{8,9},{9,10},{10,11},{11... | collective-permute-start | bytes 589832 | tf_op jit(solution)/shard_map/ppermute | solution.py:17
  26.3 25.1 %collective-permute-start = (f32[2,1,24,1024]{3,2,1,0:T(8,128)S(1)}, f32[2,1,24,1024]{3,2,1,0:T(8,128)S(1)}, u32[]{:S(2)}, u32[]{:S(2)}) collective-permute-start(f32[2,1,24,1024]{3,2,1,0:T(8,128)S(1)} %get-tuple-element.41), channel_id=1, source_target_pairs={{1,0},{2,1},{3,2},{4,3},{5,4},{6,5},{7,6},{9,8},{10,9},{11,10},{12... | collective-permute-start | bytes 589832 | tf_op jit(solution)/shard_map/ppermute | solution.py:20
  51.8 1.3 copy-start.1
  83.3 24.6 %copy-start.2 = (f32[2,6,24,1026]{3,2,1,0:T(8,128)S(1)}, f32[2,6,24,1026]{3,2,1,0:T(8,128)}, u32[]{:S(2)}) copy-start(f32[2,6,24,1026]{3,2,1,0:T(8,128)} %copy-done.1) | copy-start | bytes 3545860
  83.3 24.3 %collective-permute-start.4 = (f32[1,24,1024]{2,1,0:T(8,128)S(1)}, f32[1,24,1024]{2,1,0:T(8,128)S(1)}, u32[]{:S(2)}, u32[]{:S(2)}) collective-permute-start(f32[1,24,1024]{2,1,0:T(8,128)S(1)} %bitcast.150), channel_id=1, source_target_pairs={{1,0},{2,1},{3,2},{4,3},{5,4},{6,5},{7,6},{9,8},{10,9},{11,10},{12... | collective-permute-start | bytes 294920 | tf_op jit(solution)/shard_map/ppermute | solution.py:20
  85.1 22.5 %collective-permute-start.5 = (f32[1,24,1024]{2,1,0:T(8,128)S(1)}, f32[1,24,1024]{2,1,0:T(8,128)S(1)}, u32[]{:S(2)}, u32[]{:S(2)}) collective-permute-start(f32[1,24,1024]{2,1,0:T(8,128)S(1)} %bitcast.149), channel_id=1, source_target_pairs={{0,1},{1,2},{2,3},{3,4},{4,5},{5,6},{6,7},{8,9},{9,10},{10,11},{11... | collective-permute-start | bytes 294920 | tf_op jit(solution)/shard_map/ppermute | solution.py:17
  107.3 1.9 %copy-start.4 = (f32[1,16]{1,0:T(1,128)}, f32[1,16]{1,0:T(1,128)S(1)}, u32[]{:S(2)}) copy-start(f32[1,16]{1,0:T(1,128)S(1)} %exponential_multiply_fusion) | copy-start | bytes 196
